TPU v7x, 128 devices: a whole 4x4x4 slice. The times are simulated.
128 devices in a mesh: prow: 8 (over z, core), pcol: 16 (over x, y).
Axes of the slice: x: 4, y: 4, z: 4, core: 2. Of those that a mesh axis runs over, the one named last changes fastest.
Arguments:
- ancestor_inverse: float32 [16384, 8, 16, 128], P('prow', None, 'pcol'), as said below
- lower_panel: float32 [16384, 2048], P(('prow', 'pcol')), as said below
- structure: int32 [16, 64], replicated, may hold values from 0 to 127, as said below
- pivot_inverse: float32 [16, 128, 128], replicated, may hold values from -6 to 6
Outputs:
- panel_inverse: float32 [16384, 2048], P(('prow', 'pcol'))
- diag_inverse: float32 [16, 128, 128], replicated
Inputs may be any that keep to these rules, and one draw needn't show every extreme that they name: `structure`: each row lists 64 distinct ancestor tiles in increasing order; tiles 0 and 127 are in every row. ancestor_inverse, read as an 16384 x 16384 matrix, is symmetric. `lower_panel`: tile row j of column block b is zero unless tile j is listed in row b of structure.
All inputs are finite; a program needn't handle non-finite values.
Results may differ from a plain program's by a relative error of at most 0.000071.
Values sent between devices are 32-bit elements; how exact they have to be, the bound alone decides.
A program may use at most 128 MiB of HBM per device.

v0:
```python
import jax
import jax.numpy as jnp
from jax import lax
from jax.sharding import PartitionSpec as P

PRECISE = lax.Precision.HIGHEST


def tile_member(structure, first_row, row_count, tile_width):
    rows = first_row + jnp.arange(row_count, dtype=jnp.int32)
    tiles = rows // tile_width
    hits = structure[None, :, :] == tiles[:, None, None]
    return jnp.any(hits, axis=2).astype(jnp.float32)


def on_device(ancestor_inverse, lower_panel, structure, pivot_inverse):
    unit_rows = lower_panel.shape[0]
    tile_width = pivot_inverse.shape[1]
    descendants = structure.shape[0]
    block_rows = ancestor_inverse.shape[0]
    local_block = ancestor_inverse.reshape(
        block_rows,
        ancestor_inverse.shape[1] * ancestor_inverse.shape[2] * ancestor_inverse.shape[3],
    )
    owner_index = lax.axis_index("prow") * lax.axis_size("pcol") + lax.axis_index("pcol")
    gathered = lax.all_gather(lower_panel, "prow", axis=0, tiled=True)
    reduced = lax.psum_scatter(
        jnp.dot(local_block, gathered, precision=PRECISE, preferred_element_type=jnp.float32),
        "pcol",
        scatter_dimension=0,
        tiled=True,
    )
    membership = tile_member(structure, owner_index * unit_rows, unit_rows, tile_width)
    reduced_tiles = reduced.reshape(unit_rows, descendants, tile_width)
    panel_tiles = -(reduced_tiles * membership[:, :, None])
    local_lower = lower_panel.reshape(unit_rows, descendants, tile_width)
    correction = jnp.einsum(
        "rbi,rbj->bij",
        local_lower,
        panel_tiles,
        precision=PRECISE,
        preferred_element_type=jnp.float32,
    )
    total_correction = lax.psum(correction, ("prow", "pcol"))
    return (
        panel_tiles.reshape(unit_rows, descendants * tile_width),
        pivot_inverse - total_correction,
    )


def solution(mesh):
    return jax.shard_map(
        on_device,
        mesh=mesh,
        in_specs=(P("prow", None, "pcol", None), P(("prow", "pcol"), None), P(), P()),
        out_specs=(P(("prow", "pcol"), None), P()),
        check_vma=False,
    )
```

profile of v0, /device:TPU:1, one launch (start us, length us, event | category | flops | bytes accessed | tf_op | source)
XLA Modules:
  0.0 399.1 jit_solution(6475974717212178277)
XLA Ops:
  7.2 0.0 all-gather.2.cloned.1.call-start
  7.2 0.7 all-gather.2.cloned.1.call-update
  7.9 0.0 reduce-scatter.2.cloned.1.call-start
  7.9 55.4 %all-gather.2.cloned.1.call-done = f32[1024,2048]{1,0:T(8,128)} async-done(((f32[128,2048]{1,0:T(8,128)}), f32[1024,2048]{1,0:T(8,128)}) %all-gather.2.cloned.1.call-update) | async-done | bytes 8388624 | tf_op jit(solution)/shard_map/all_gather | solution.py:26
  63.3 63.2 %fusion = f32[2048,2048]{1,0:T(8,128)} fusion(f32[1024,2048]{1,0:T(8,128)} %all-gather.2.cloned.1.call-done, f32[256,8,8,128]{3,2,1,0:T(8,128)} %bitcast.20), kind=kOutput, calls=%fused_computation | convolution fusion | flops 51539607552 | bytes 33554432 | tf_op jit(solution)/shard_map/dot_general | solution.py:28
  126.5 0.0 copy-start.1
  126.5 0.0 copy-start
  126.5 0.0 reduce-scatter.2.cloned.1.call-update
  126.5 0.0 all-reduce.2.cloned.1.call-start
  126.6 0.6 copy-done.1
  127.2 0.2 compare_reduce_fusion
  127.4 0.1 mul.21
  127.5 0.3 copy.16
  127.8 1.6 copy.14
  129.4 107.0 %reduce-scatter.2.cloned.1.call-done = f32[128,2048]{1,0:T(8,128)} async-done(((f32[2048,2048]{1,0:T(8,128)}), f32[128,2048]{1,0:T(8,128)}) %reduce-scatter.2.cloned.1.call-update) | async-done | bytes 1048592 | tf_op jit(solution)/shard_map/reduce_scatter | solution.py:27
  236.4 2.5 copy.17
  239.0 0.0 copy-done
  239.0 3.4 convolution_bitcast_fusion
  242.4 0.0 all-reduce.2.cloned.1.call-update
  242.4 2.3 multiply_negate_fusion
  244.7 145.2 %all-reduce.2.cloned.1.call-done = f32[16,128,128]{1,2,0:T(8,128)} async-done(((f32[16,128,128]{1,2,0:T(8,128)}), f32[16,128,128]{1,2,0:T(8,128)}) %all-reduce.2.cloned.1.call-update) | async-done | bytes 1048592 | tf_op jit(solution)/shard_map/psum | solution.py:44
  389.9 1.3 sub.10
  391.3 1.3 copy.15
  (2 shorter events, 0.0 us)
Async XLA Ops:
  7.2 56.2 %all-gather.2.cloned.1.call-start = ((), (), s32[]{:S(2)}) async-start(), calls=%async_computation.1 | async-start | bytes 9437184 | tf_op jit(solution)/shard_map/all_gather | solution.py:26
  7.9 228.5 %reduce-scatter.2.cloned.1.call-start = ((), (), s32[]{:S(2)}) async-start(), calls=%async_computation.2 | async-start | bytes 17825792 | tf_op jit(solution)/shard_map/reduce_scatter | solution.py:27
  126.5 0.7 copy-start.1
  126.5 112.5 %copy-start = (f32[128,2048]{1,0:T(8,128)S(1)}, f32[128,2048]{1,0:T(8,128)}, u32[]{:S(2)}) copy-start(f32[128,2048]{1,0:T(8,128)} %param.5) | copy-start | bytes 3145732
  126.5 263.4 %all-reduce.2.cloned.1.call-start = ((), (), s32[]{:S(2)}) async-start(), calls=%async_computation.3 | async-start | bytes 2097152 | tf_op jit(solution)/shard_map/psum | solution.py:44
Sparse Core Ops, SparseCore 0:
  9.7 53.5 all-gather.1
  126.6 109.7 reduce-scatter.1
  242.5 147.3 all-reduce.1
where the time goes:
time: 399 us
  waiting for transfers between devices  308 us (77%)
  matrix products  66.6 us (17%)
  between operations  13.8 us (3%)
  local copies, waits for them, and re-layouts  6.4 us (2%)
    psum x1, waiting for transfers between devices, on_device(): total_correction = lax.psum(correction, ('prow', 'pcol'))  145 us
    reduce_scatter x1, waiting for transfers between devices, on_device(): lax.psum_scatter(jnp.dot(local_block, gathered, precision=PRECISE, prefer...  107 us
    dot_general x1, matrix products, on_device(): jnp.dot(local_block, gathered, precision=PRECISE, preferred_element_type=...  63.2 us
    all_gather x1, waiting for transfers between devices, on_device(): gathered = lax.all_gather(lower_panel, 'prow', axis=0, tiled=True)  55.4 us
  transfers between devices with their start and end apart: 3, of which 3 were waited for; matrix products, arithmetic and copies ran while one was open for 1% of the time, Pallas kernels for 0%

commit v1 on v0

v1 whole, which is shorter than its diff:
```python
import jax
import jax.numpy as jnp
from jax import lax
from jax.experimental import pallas as pl
from jax.experimental.pallas import tpu as pltpu
from jax.sharding import PartitionSpec as P

F32 = jnp.float32
BF16 = jnp.bfloat16
MESH = pl.DeviceIdType.MESH
W = 128
NP = 8
RING = 4
PAIRS = 8
COLS = 2 * W


def split(value):
    high = value.astype(BF16)
    low = (value - high.astype(F32)).astype(BF16)
    return high, low


def kernel(
    a_hbm, lower_ref, structure_ref, pivot_ref, panel_hbm, diag_hbm,
    a_high, a_low, b_high, b_low, mask, gathered, partial,
    far, near, far_tile, near_tile, panel, correction,
    prow_in, prow_sum, x_in, y_in, diag,
    a_sem, out_sem, gather_send, gather_recv, scatter_send, scatter_recv,
    reduce_send, reduce_recv,
):
    prow, pcol = lax.axis_index("prow"), lax.axis_index("pcol")
    z, core = prow // 2, prow % 2
    x, y = pcol // RING, pcol % RING

    def along_x(step):
        return (prow, ((x + step) % RING) * RING + y)

    def along_y(step):
        return (prow, x * RING + (y + step) % RING)

    def along_prow(step):
        return ((prow + step) % NP, pcol)

    def tile_of(step, which):
        return ((z + step) % RING) * 2 + which

    sibling = (tile_of(0, 1 - core), pcol)
    z_next = (tile_of(1, core), pcol)
    z_last = (tile_of(3, core), pcol)

    def send(source, target, send_sem, recv_sem, device):
        pltpu.make_async_remote_copy(
            src_ref=source, dst_ref=target, send_sem=send_sem, recv_sem=recv_sem,
            device_id=device, device_id_type=MESH,
        ).start()

    def await_bytes(ref, sem):
        pltpu.make_async_copy(ref, ref, sem).wait()

    for part in range(8):
        pltpu.make_async_copy(a_hbm.at[part], partial.at[part], a_sem.at[part]).start()

    own = lower_ref[...]
    for pair in range(PAIRS):
        gathered[pair, prow] = own[:, pair * COLS:(pair + 1) * COLS]
    listed = jnp.where(structure_ref[...] == prow * 16 + pcol, 1.0, 0.0).astype(F32)
    mask[...] = jnp.broadcast_to(jnp.max(listed, axis=1, keepdims=True), mask.shape)

    barrier = pltpu.get_barrier_semaphore()
    partners = [along_prow(k) for k in range(1, NP)]
    partners += [along_x(k) for k in range(1, RING)]
    partners += [along_y(k) for k in range(1, RING)]
    for device in partners:
        pl.semaphore_signal(barrier, inc=1, device_id=device, device_id_type=MESH)
    pl.semaphore_wait(barrier, len(partners))

    def gather_send_to(t, ref, which, device):
        send(ref, ref, gather_send.at[t, which], gather_recv.at[t, which], device)

    half = W // 2

    def gather_first(t):
        ref = gathered.at[t, prow]
        gather_send_to(t, ref, 0, z_next)
        gather_send_to(t, ref, 1, z_last)
        gather_send_to(t, ref, 2, sibling)

    def gather_second(t):
        ref = gathered.at[t, tile_of(3, core)]
        await_bytes(ref, gather_recv.at[t, 0])
        gather_send_to(t, ref.at[pl.ds(0, half)], 5, z_next)
        gather_send_to(t, ref, 3, sibling)
        ref = gathered.at[t, tile_of(1, core)]
        await_bytes(ref, gather_recv.at[t, 1])
        gather_send_to(t, ref.at[pl.ds(half, half)], 6, z_last)
        gather_send_to(t, ref, 4, sibling)

    def gather_third(t):
        ref = gathered.at[t, tile_of(2, core)]
        await_bytes(ref.at[pl.ds(0, half)], gather_recv.at[t, 5])
        await_bytes(ref.at[pl.ds(half, half)], gather_recv.at[t, 6])
        gather_send_to(t, ref, 7, sibling)
        for which, step in ((2, 0), (3, 3), (4, 1), (7, 2)):
            await_bytes(gathered.at[t, tile_of(step, 1 - core)], gather_recv.at[t, which])

    def multiply(t):
        for tile in range(NP):
            high, low = split(gathered[t, tile])
            b_high[tile * W:(tile + 1) * W] = high
            b_low[tile * W:(tile + 1) * W] = low

        @pl.loop(0, RING)
        def _(i):
            rows = pl.ds(pl.multiple_of(i * 4 * W, 4 * W), 4 * W)
            total = jnp.dot(a_high[rows], b_high[...], preferred_element_type=F32)
            total += jnp.dot(a_low[rows], b_high[...], preferred_element_type=F32)
            total += jnp.dot(a_high[rows], b_low[...], preferred_element_type=F32)
            for j in range(RING):
                block = total[j * W:(j + 1) * W]
                partial[2 * t, i, j] = block[:, :W]
                partial[2 * t + 1, j, i] = block[:, W:]

    def routes(t):
        return (
            (2 * t, x, y, along_x, along_y),
            (2 * t + 1, y, x, along_y, along_x),
        )

    def scatter_send_to(b, which, source, target, device):
        send(source, target, scatter_send.at[b, which], scatter_recv.at[b, which], device)

    def scatter_first(t):
        for b, u, v, first, second in routes(t):
            block = partial.at[b, (u + 2) % RING]
            scatter_send_to(b, 0, block.at[pl.ds(0, 2)], far.at[b, 0], first(1))
            scatter_send_to(b, 1, block.at[pl.ds(2, 2)], far.at[b, 1], first(3))

    def scatter_second(t):
        for b, u, v, first, second in routes(t):
            up, down = (u + 1) % RING, (u + 3) % RING
            await_bytes(far.at[b, 0], scatter_recv.at[b, 0])
            partial[b, up, 0:2] += far[b, 0]
            scatter_send_to(b, 2, partial.at[b, up], near.at[b, 0], first(1))
            await_bytes(far.at[b, 1], scatter_recv.at[b, 1])
            partial[b, down, 2:4] += far[b, 1]
            scatter_send_to(b, 3, partial.at[b, down], near.at[b, 1], first(3))

    def scatter_third(t):
        for b, u, v, first, second in routes(t):
            await_bytes(near.at[b, 0], scatter_recv.at[b, 2])
            await_bytes(near.at[b, 1], scatter_recv.at[b, 3])
            partial[b, u] += near[b, 0] + near[b, 1]
            block = partial.at[b, u, (v + 2) % RING]
            scatter_send_to(b, 4, block.at[pl.ds(0, half)], far_tile.at[b, 0], second(1))
            scatter_send_to(b, 5, block.at[pl.ds(half, half)], far_tile.at[b, 1], second(3))

    def scatter_fourth(t):
        for b, u, v, first, second in routes(t):
            up, down = (v + 1) % RING, (v + 3) % RING
            await_bytes(far_tile.at[b, 0], scatter_recv.at[b, 4])
            partial[b, u, up, 0:half] += far_tile[b, 0]
            scatter_send_to(b, 6, partial.at[b, u, up], near_tile.at[b, 0], second(1))
            await_bytes(far_tile.at[b, 1], scatter_recv.at[b, 5])
            partial[b, u, down, half:W] += far_tile[b, 1]
            scatter_send_to(b, 7, partial.at[b, u, down], near_tile.at[b, 1], second(3))

    def columns(t):
        return pl.ds(pl.multiple_of(t * COLS, COLS), COLS)

    def finish(t):
        for h, (b, u, v, first, second) in enumerate(routes(t)):
            await_bytes(near_tile.at[b, 0], scatter_recv.at[b, 6])
            await_bytes(near_tile.at[b, 1], scatter_recv.at[b, 7])
            product = partial[b, u, v] + near_tile[b, 0] + near_tile[b, 1]
            block = -(product * mask[pl.ds(b, 1), :])
            panel[t, :, h * W:(h + 1) * W] = block
            correction[t, h * W:(h + 1) * W] = lax.dot_general(
                gathered[t, prow, :, h * W:(h + 1) * W], block,
                (((0,), (0,)), ((), ())),
                precision=lax.Precision.HIGHEST, preferred_element_type=F32,
            )
        pltpu.make_async_copy(panel.at[t], panel_hbm.at[:, columns(t)], out_sem.at[0, t]).start()
        for k in range(1, NP):
            rows = pl.ds(pl.multiple_of(((prow + k) % NP) * 32, 32), 32)
            send(correction.at[t, rows], prow_in.at[t, k],
                 reduce_send.at[t, 0], reduce_recv.at[t, 0], along_prow(k))

    own_rows = pl.ds(pl.multiple_of(prow * 32, 32), 32)
    final_rows = pl.ds(pl.multiple_of(prow * 32 + x * 8, 8), 8)

    def reduce_second(t):
        await_bytes(prow_in.at[t, pl.ds(1, NP - 1)], reduce_recv.at[t, 0])
        total = correction[t, own_rows]
        for k in range(1, NP):
            total += prow_in[t, k]
        prow_sum[t] = total
        for k in range(1, RING):
            rows = pl.ds(pl.multiple_of(((x + k) % RING) * 8, 8), 8)
            send(prow_sum.at[t, rows], x_in.at[t, k],
                 reduce_send.at[t, 1], reduce_recv.at[t, 1], along_x(k))

    def reduce_third(t):
        await_bytes(x_in.at[t, pl.ds(1, RING - 1)], reduce_recv.at[t, 1])
        total = prow_sum[t, pl.ds(pl.multiple_of(x * 8, 8), 8)]
        for k in range(1, RING):
            total += x_in[t, k]
        y_in[t, y] = total
        for k in range(1, RING):
            send(y_in.at[t, y], y_in.at[t, y],
                 reduce_send.at[t, 2], reduce_recv.at[t, 2], along_y(k))

    def reduce_fourth(t):
        await_bytes(y_in.at[t, pl.ds(0, RING - 1)], reduce_recv.at[t, 2])
        total = (y_in[t, 0] + y_in[t, 1]) + (y_in[t, 2] + y_in[t, 3])
        rows = pl.ds(pl.multiple_of(t * COLS + prow * 32 + x * 8, 8), 8)
        diag[t, final_rows] = pivot_ref[rows] - total
        for k in range(1, RING):
            send(diag.at[t, final_rows], diag.at[t, final_rows],
                 reduce_send.at[t, 3], reduce_recv.at[t, 3], along_x(k))

    def reduce_fifth(t):
        await_bytes(diag.at[t, pl.ds(0, 24)], reduce_recv.at[t, 3])
        for k in range(1, NP):
            send(diag.at[t, own_rows], diag.at[t, own_rows],
                 reduce_send.at[t, 4], reduce_recv.at[t, 4], along_prow(k))

    def reduce_last(t):
        await_bytes(diag.at[t, pl.ds(0, 224)], reduce_recv.at[t, 4])
        rows = pl.ds(pl.multiple_of(t * COLS, COLS), COLS)
        pltpu.make_async_copy(diag.at[t], diag_hbm.at[rows], out_sem.at[1, t]).start()

    gather_first(0)

    for part in range(8):
        await_bytes(partial.at[part], a_sem.at[part])

        @pl.loop(0, 16)
        def _(i):
            rows = pl.ds(pl.multiple_of(part * 256 + i * 16, 16), 16)
            for r in range(NP):
                high, low = split(partial[part, i // 4, i % 4, pl.ds(r, 16, stride=8), :])
                a_high[rows, r * W:(r + 1) * W] = high
                a_low[rows, r * W:(r + 1) * W] = low

    @pl.loop(0, 20)
    def _(step):
        def at(lag, body):
            t = step - lag

            @pl.when((t >= 0) & (t < PAIRS))
            def _():
                body(t)

        at(4, scatter_second)
        at(5, scatter_third)
        at(6, scatter_fourth)
        at(7, finish)
        at(8, reduce_second)
        at(9, reduce_third)
        at(10, reduce_fourth)
        at(11, reduce_fifth)
        at(12, reduce_last)
        at(2, gather_third)
        at(2, multiply)
        at(2, scatter_first)
        at(1, gather_second)

        @pl.when(step + 1 < PAIRS)
        def _():
            gather_first(step + 1)

    @pl.loop(0, PAIRS)
    def _(t):
        for which in range(8):
            ref = gathered.at[t, 0]
            await_bytes(ref.at[pl.ds(0, half)] if which in (5, 6) else ref, gather_send.at[t, which])
        for b in (2 * t, 2 * t + 1):
            for which in range(8):
                buffer = (far, near, far_tile, near_tile)[which // 2]
                await_bytes(buffer.at[b, which % 2], scatter_send.at[b, which])
        await_bytes(prow_in.at[t, pl.ds(1, NP - 1)], reduce_send.at[t, 0])
        await_bytes(x_in.at[t, pl.ds(1, RING - 1)], reduce_send.at[t, 1])
        await_bytes(y_in.at[t, pl.ds(0, RING - 1)], reduce_send.at[t, 2])
        await_bytes(diag.at[t, pl.ds(0, 24)], reduce_send.at[t, 3])
        await_bytes(diag.at[t, pl.ds(0, 224)], reduce_send.at[t, 4])
        await_bytes(panel.at[t], out_sem.at[0, t])
        await_bytes(diag.at[t], out_sem.at[1, t])


def on_device(ancestor_inverse, lower_panel, structure, pivot_inverse):
    rows = ancestor_inverse.shape[0]
    blocks = ancestor_inverse.reshape(8, 4, 4, W, W)
    pivot_rows = pivot_inverse.reshape(16 * W, W)
    vmem = pl.BlockSpec(memory_space=pltpu.VMEM)
    hbm = pl.BlockSpec(memory_space=pl.ANY)
    depth = NP * W
    dma = pltpu.SemaphoreType.DMA
    panel, diag = pl.pallas_call(
        kernel,
        out_shape=(
            jax.ShapeDtypeStruct(lower_panel.shape, F32),
            jax.ShapeDtypeStruct(pivot_rows.shape, F32),
        ),
        in_specs=[hbm, vmem, vmem, vmem],
        out_specs=(hbm, hbm),
        scratch_shapes=[
            pltpu.VMEM((rows, depth), BF16),
            pltpu.VMEM((rows, depth), BF16),
            pltpu.VMEM((depth, COLS), BF16),
            pltpu.VMEM((depth, COLS), BF16),
            pltpu.VMEM((16, W), F32),
            pltpu.VMEM((PAIRS, NP, W, COLS), F32),
            pltpu.VMEM((16, RING, RING, W, W), F32),
            pltpu.VMEM((16, 2, 2, W, W), F32),
            pltpu.VMEM((16, 2, 4, W, W), F32),
            pltpu.VMEM((16, 2, W // 2, W), F32),
            pltpu.VMEM((16, 2, W, W), F32),
            pltpu.VMEM((PAIRS, W, COLS), F32),
            pltpu.VMEM((PAIRS, COLS, W), F32),
            pltpu.VMEM((PAIRS, NP, 32, W), F32),
            pltpu.VMEM((PAIRS, 32, W), F32),
            pltpu.VMEM((PAIRS, RING, 8, W), F32),
            pltpu.VMEM((PAIRS, RING, 8, W), F32),
            pltpu.VMEM((PAIRS, COLS, W), F32),
            dma((8,)),
            dma((2, PAIRS)),
            dma((PAIRS, 8)),
            dma((PAIRS, 8)),
            dma((16, 8)),
            dma((16, 8)),
            dma((PAIRS, 5)),
            dma((PAIRS, 5)),
        ],
        compiler_params=pltpu.CompilerParams(
            collective_id=0, has_side_effects=True, vmem_limit_bytes=62 * 1024 * 1024,
        ),
        cost_estimate=pl.CostEstimate(
            flops=2 * 3 * rows * depth * lower_panel.shape[1], bytes_accessed=12 << 20, transcendentals=0,
        ),
    )(blocks, lower_panel, structure, pivot_rows)
    return panel, diag.reshape(pivot_inverse.shape)


def solution(mesh):
    return jax.shard_map(
        on_device,
        mesh=mesh,
        in_specs=(P("prow", None, "pcol", None), P(("prow", "pcol"), None), P(), P()),
        out_specs=(P(("prow", "pcol"), None), P()),
        check_vma=False,
    )
```

time: 399 us -> 152 us (0.38)
  waiting for transfers between devices: 308 us -> 0 us
  Pallas kernels: 0 us -> 146 us
  matrix products: 66.6 us -> 0 us
  between operations: 13.8 us -> 0.64 us
    pallas_call x0 -> x1, Pallas kernels: none -> 146 us  [on_device(): pl.pallas_call(kernel, out_shape=(jax.ShapeDtypeStruct(lower_panel.shape,...]
    psum x1 -> x0, waiting for transfers between devices: 145 us -> none  [on_device(): total_correction = lax.psum(correction, ('prow', 'pcol'))]
    reduce_scatter x1 -> x0, waiting for transfers between devices: 107 us -> none  [on_device(): lax.psum_scatter(jnp.dot(local_block, gathered, precision=PRECISE, prefer...]
    dot_general x2 -> x0, matrix products: 66.6 us -> none  [the longest x1 63.2 us: on_device(): jnp.dot(local_block, gathered, precision=PRECISE, preferred_element_type=...]
    all_gather x1 -> x0, waiting for transfers between devices: 55.4 us -> none  [on_device(): gathered = lax.all_gather(lower_panel, 'prow', axis=0, tiled=True)]
  transfers between devices with their start and end apart: 3 -> 0, of which waited for: 3 -> 0; matrix products, arithmetic and copies ran while one was open for 1% -> 0% of each run, Pallas kernels for 0% -> 0%
where the time goes in v1:
time: 152 us
  Pallas kernels  146 us (96%)
  local copies, waits for them, and re-layouts  4.59 us (3%)
    pallas_call x1, Pallas kernels, on_device(): pl.pallas_call(kernel, out_shape=(jax.ShapeDtypeStruct(lower_panel.shape,...  146 us
    unnamed x2, local copies, waits for them, and re-layouts  4.59 us

profile of v1, /device:TPU:1, one launch (start us, length us, event | category | flops | bytes accessed | tf_op | source)
XLA Modules:
  0.0 151.6 jit_solution(14027534027173687200)
XLA Ops:
  0.6 146.3 %shard_map.59 = (f32[128,2048]{1,0:T(8,128)}, f32[2048,128]{1,0:T(8,128)}) custom-call(f32[8,4,4,128,128]{4,3,2,1,0:T(8,128)} %bitcast.4, f32[128,2048]{1,0:T(8,128)} %lower_ref.1, s32[16,64]{1,0:T(8,128)} %structure_ref.1, f32[2048,128]{1,0:T(8,128)} %bitcast.5), custom_call_target="tpu_custom_call" | custom-call | flops 25769803776 | bytes 12582912 | tf_op jit(solution)/shard_map/pallas_call | solution.py:299
  147.0 2.3 %copy.8 = f32[128,2048]{1,0:T(8,128)} copy(f32[128,2048]{1,0:T(8,128)} %get-tuple-element.8) | data formatting | bytes 2097152
  149.3 2.3 %copy.9 = f32[16,128,128]{2,1,0:T(8,128)} copy(f32[16,128,128]{2,1,0:T(8,128)} %bitcast.3) | data formatting | bytes 2097152

commit v2 on v1

v2 whole, which is shorter than its diff:
```python
import jax
import jax.numpy as jnp
from jax import lax
from jax.experimental import pallas as pl
from jax.experimental.pallas import tpu as pltpu
from jax.sharding import PartitionSpec as P

F32 = jnp.float32
BF16 = jnp.bfloat16
MESH = pl.DeviceIdType.MESH
W = 128
HALF = W // 2
NP = 8
RING = 4
PAIRS = 8
LAST = PAIRS - 1
COLS = 2 * W
EARLY = 2
LATE = 2
MIDDLE = 4


def split(value):
    high = value.astype(BF16)
    low = (value - high.astype(F32)).astype(BF16)
    return high, low


def aligned(start, size):
    return pl.ds(pl.multiple_of(start, size), size)


def kernel(
    a_hbm, lower_hbm, structure_ref, pivot_hbm, panel_hbm, diag_hbm,
    a_high, a_low, b_high, b_low, mask, ring_mask, gathered, partial,
    far, near, far_tile, near_tile, panel, correction, ring_lower, ring_panel,
    prow_in, x_in, y_in, pivot, diag,
    a_sem, lower_sem, pivot_sem, out_sem, gather_send, gather_recv,
    scatter_send, scatter_recv, reduce_send, reduce_recv, ring_sem,
):
    prow, pcol = lax.axis_index("prow"), lax.axis_index("pcol")
    z, core = prow // 2, prow % 2
    x, y = pcol // RING, pcol % RING

    def along_x(step):
        return (prow, ((x + step) % RING) * RING + y)

    def along_y(step):
        return (prow, x * RING + (y + step) % RING)

    def along_prow(step):
        return ((prow + step) % NP, pcol)

    def tile_of(step, which):
        return ((z + step) % RING) * 2 + which

    sibling = (tile_of(0, 1 - core), pcol)
    z_next = (tile_of(1, core), pcol)
    z_last = (tile_of(3, core), pcol)

    def send(source, target, send_sem, recv_sem, device):
        pltpu.make_async_remote_copy(
            src_ref=source, dst_ref=target, send_sem=send_sem, recv_sem=recv_sem,
            device_id=device, device_id_type=MESH,
        ).start()

    def await_bytes(ref, sem):
        pltpu.make_async_copy(ref, ref, sem).wait()

    barrier = pltpu.get_barrier_semaphore()
    partners = [along_prow(k) for k in range(1, NP)]
    partners += [along_x(k) for k in range(1, RING)]
    partners += [along_y(k) for k in range(1, RING)]
    for device in partners:
        pl.semaphore_signal(barrier, inc=1, device_id=device, device_id_type=MESH)

    for t in range(PAIRS):
        pltpu.make_async_copy(
            lower_hbm.at[:, pl.ds(t * COLS, COLS)], gathered.at[t, prow], lower_sem.at[min(t, 1)]
        ).start()
    for part in range(4):
        pltpu.make_async_copy(
            a_hbm.at[pl.ds(2 * part, 2)], partial.at[pl.ds(2 * part, 2)], a_sem.at[part]
        ).start()
    own_rows = aligned(prow * 32, 32)
    pltpu.make_async_copy(pivot_hbm.at[:, own_rows], pivot, pivot_sem).start()

    def member(tile):
        listed = jnp.where(structure_ref[...] == prow * 16 + tile, 1.0, 0.0).astype(F32)
        return jnp.broadcast_to(jnp.max(listed, axis=1, keepdims=True), mask.shape)

    mask[...] = member(pcol)
    for k in range(RING):
        ring_mask[0, k] = member(x * RING + k)
        ring_mask[1, k] = member(k * RING + y)

    await_bytes(gathered.at[0, prow], lower_sem.at[0])
    pl.semaphore_wait(barrier, len(partners))

    def gather_send_to(t, ref, which, recv, device):
        send(ref, ref, gather_send.at[which], recv, device)

    def gather_first(t):
        ref = gathered.at[t, prow]
        gather_send_to(t, ref, 0, gather_recv.at[t, 0], z_next)
        gather_send_to(t, ref, 1, gather_recv.at[t, 1], z_last)
        gather_send_to(t, ref, 2, gather_recv.at[t, 3], sibling)

    def gather_second(t):
        ref = gathered.at[t, tile_of(3, core)]
        await_bytes(ref, gather_recv.at[t, 0])
        gather_send_to(t, ref.at[pl.ds(0, HALF)], 5, gather_recv.at[t, 2], z_next)
        gather_send_to(t, ref, 3, gather_recv.at[t, 4], sibling)
        ref = gathered.at[t, tile_of(1, core)]
        await_bytes(ref, gather_recv.at[t, 1])
        gather_send_to(t, ref.at[pl.ds(HALF, HALF)], 6, gather_recv.at[t, 2], z_last)
        gather_send_to(t, ref, 4, gather_recv.at[t, 5], sibling)

    def gather_third(t):
        ref = gathered.at[t, tile_of(2, core)]
        await_bytes(ref, gather_recv.at[t, 2])
        gather_send_to(t, ref, 7, gather_recv.at[t, 6], sibling)

    def gather_wait(t):
        for k, step in enumerate((0, 3, 1, 2)):
            await_bytes(gathered.at[t, tile_of(step, 1 - core)], gather_recv.at[t, 3 + k])

    def multiply(t):
        for tile in range(NP):
            high, low = split(gathered[t, tile])
            b_high[tile * W:(tile + 1) * W] = high
            b_low[tile * W:(tile + 1) * W] = low

        @pl.loop(0, RING)
        def _(i):
            rows = aligned(i * 4 * W, 4 * W)
            total = jnp.dot(a_high[rows], b_high[...], preferred_element_type=F32)
            total += jnp.dot(a_low[rows], b_high[...], preferred_element_type=F32)
            total += jnp.dot(a_high[rows], b_low[...], preferred_element_type=F32)
            for j in range(RING):
                block = total[j * W:(j + 1) * W]
                partial[2 * t, i, j] = block[:, :W]
                partial[2 * t + 1, j, i] = block[:, W:]

    def multiply_first():
        @pl.loop(0, RING)
        def _(k):
            step = jnp.where(k == 0, 0, jnp.where(k == 1, 3, jnp.where(k == 2, 1, 2)))

            @pl.when(k == 3)
            def _():
                gather_third(0)

            chip = (z + step) % RING
            depth = aligned(chip * COLS, COLS)
            await_bytes(gathered.at[0, chip * 2 + 1 - core], gather_recv.at[0, 3 + k])
            for which in range(2):
                high, low = split(gathered[0, chip * 2 + which])
                b_high[which * W:(which + 1) * W] = high
                b_low[which * W:(which + 1) * W] = low

            @pl.loop(0, RING)
            def _(i):
                rows = aligned(i * 4 * W, 4 * W)
                high, low = b_high[0:COLS], b_low[0:COLS]
                total = jnp.dot(a_high[rows, depth], high, preferred_element_type=F32)
                total += jnp.dot(a_low[rows, depth], high, preferred_element_type=F32)
                total += jnp.dot(a_high[rows, depth], low, preferred_element_type=F32)
                for j in range(RING):
                    block = total[j * W:(j + 1) * W]
                    partial[0, i, j] = block[:, :W] + jnp.where(k == 0, 0.0, partial[0, i, j])
                    partial[1, j, i] = block[:, W:] + jnp.where(k == 0, 0.0, partial[1, j, i])

    def routes(t):
        return (
            (2 * t, x, y, along_x, along_y),
            (2 * t + 1, y, x, along_y, along_x),
        )

    def scatter_send_to(t, which, source, target, device):
        send(source, target, scatter_send.at[which], scatter_recv.at[t, which // 2], device)

    def scatter_first(t):
        for b, u, v, first, second in routes(t):
            block = partial.at[b, (u + 2) % RING]
            scatter_send_to(t, 0, block.at[pl.ds(0, 2)], far.at[b, 0], first(1))
            scatter_send_to(t, 1, block.at[pl.ds(2, 2)], far.at[b, 1], first(3))

    def scatter_second(t):
        await_bytes(far.at[pl.ds(2 * t, 2)], scatter_recv.at[t, 0])
        for b, u, v, first, second in routes(t):
            up, down = (u + 1) % RING, (u + 3) % RING
            partial[b, up, 0:2] += far[b, 0]
            scatter_send_to(t, 2, partial.at[b, up], near.at[b, 0], first(1))
            partial[b, down, 2:4] += far[b, 1]
            scatter_send_to(t, 3, partial.at[b, down], near.at[b, 1], first(3))

    def scatter_third(t):
        await_bytes(near.at[pl.ds(2 * t, 2)], scatter_recv.at[t, 1])
        for b, u, v, first, second in routes(t):
            partial[b, u] += near[b, 0] + near[b, 1]

    def scatter_turn(t):
        for b, u, v, first, second in routes(t):
            block = partial.at[b, u, (v + 2) % RING]
            scatter_send_to(t, 4, block.at[pl.ds(0, HALF)], far_tile.at[b, 0], second(1))
            scatter_send_to(t, 5, block.at[pl.ds(HALF, HALF)], far_tile.at[b, 1], second(3))

    def scatter_fourth(t):
        await_bytes(far_tile.at[pl.ds(2 * t, 2)], scatter_recv.at[t, 2])
        for b, u, v, first, second in routes(t):
            up, down = (v + 1) % RING, (v + 3) % RING
            partial[b, u, up, 0:HALF] += far_tile[b, 0]
            scatter_send_to(t, 6, partial.at[b, u, up], near_tile.at[b, 0], second(1))
            partial[b, u, down, HALF:W] += far_tile[b, 1]
            scatter_send_to(t, 7, partial.at[b, u, down], near_tile.at[b, 1], second(3))

    def finish(t):
        await_bytes(near_tile.at[pl.ds(2 * t, 2)], scatter_recv.at[t, 3])
        for h, (b, u, v, first, second) in enumerate(routes(t)):
            product = partial[b, u, v] + near_tile[b, 0] + near_tile[b, 1]
            panel[t, :, h * W:(h + 1) * W] = -(product * mask[pl.ds(b, 1), :])
        columns = aligned(t * COLS, COLS)
        pltpu.make_async_copy(panel.at[t], panel_hbm.at[:, columns], out_sem.at[0]).start()

    def correct(t):
        for h in range(2):
            correction[t, h * W:(h + 1) * W] = lax.dot_general(
                gathered[t, prow, :, h * W:(h + 1) * W], panel[t, :, h * W:(h + 1) * W],
                (((0,), (0,)), ((), ())),
                precision=lax.Precision.HIGHEST, preferred_element_type=F32,
            )

    def ring_send():
        for t in range(EARLY, PAIRS):
            for h, (step, slot) in enumerate(((along_y, y), (along_x, x))):
                source = gathered.at[t, prow, :, pl.ds(h * W, W)]
                ring_lower[t - EARLY, h, slot] = source[...]
                for k in range(1, RING):
                    send(source, ring_lower.at[t - EARLY, h, slot], ring_sem.at[0], ring_sem.at[1], step(k))

    def correct_early(t):
        for h, (b, u, v, first, second) in enumerate(routes(t)):
            for k in range(RING):
                ring_panel[k] = -(partial[b, u, k] * ring_mask[h, k, pl.ds(b, 1), :])
            correction[t, h * W:(h + 1) * W] = lax.dot_general(
                ring_lower[t - EARLY, h].reshape(RING * W, W), ring_panel[...].reshape(RING * W, W),
                (((0,), (0,)), ((), ())),
                precision=lax.Precision.HIGHEST, preferred_element_type=F32,
            )

    def reduce_send_to(t, stage, source, target, device):
        send(source, target, reduce_send.at[stage], reduce_recv.at[t, stage], device)

    def reduce_first(t):
        for k in range(1, NP):
            rows = aligned(((prow + k) % NP) * 32, 32)
            reduce_send_to(t, 0, correction.at[t, rows], prow_in.at[k, t], along_prow(k))

    def reduce_second(t):
        await_bytes(prow_in.at[pl.ds(1, NP - 1), t], reduce_recv.at[t, 0])
        total = correction[t, own_rows]
        for k in range(1, NP):
            total += prow_in[k, t]
        x_in[x, t] = total
        for k in range(1, RING):
            ref = x_in.at[x, t]
            reduce_send_to(t, 1, ref, ref, along_x(k))

    def reduce_third(t):
        await_bytes(x_in.at[pl.ds(0, RING - 1), t], reduce_recv.at[t, 1])
        y_in[y, t] = (x_in[0, t] + x_in[1, t]) + (x_in[2, t] + x_in[3, t])
        for k in range(1, RING):
            ref = y_in.at[y, t]
            reduce_send_to(t, 2, ref, ref, along_y(k))

    def reduce_fourth(t):
        await_bytes(y_in.at[pl.ds(0, RING - 1), t], reduce_recv.at[t, 2])
        total = (y_in[0, t] + y_in[1, t]) + (y_in[2, t] + y_in[3, t])
        diag[t, own_rows] = pivot[t] - total
        for k in range(1, NP):
            ref = diag.at[t, own_rows]
            reduce_send_to(t, 3, ref, ref, along_prow(k))

    def reduce_last(t):
        await_bytes(diag.at[t, pl.ds(0, 224)], reduce_recv.at[t, 3])
        pltpu.make_async_copy(diag.at[t], diag_hbm.at[t], out_sem.at[1]).start()

    def prepare():
        await_bytes(gathered.at[pl.ds(1, PAIRS - 1), prow], lower_sem.at[1])
        ring_send()

        @pl.loop(0, 128)
        def _(i):
            part = i // 32

            @pl.when(i % 32 == 0)
            def _():
                await_bytes(partial.at[pl.ds(2 * part, 2)], a_sem.at[part])

            rows = aligned(i * 16, 16)
            for r in range(NP):
                high, low = split(partial[i // 16, (i // 4) % 4, i % 4, pl.ds(r, 16, stride=8), :])
                a_high[rows, r * W:(r + 1) * W] = high
                a_low[rows, r * W:(r + 1) * W] = low

        await_bytes(pivot, pivot_sem)

    @pl.loop(-2, PAIRS + 7)
    def _(step):
        def at(lag, body, first=0, end=PAIRS):
            t = step - lag

            @pl.when((t >= first) & (t < end))
            def _():
                body(t)

        def once(when, body, *args):
            @pl.when(step == when)
            def _():
                body(*args)

        def late(when, body, first=LATE, end=PAIRS):
            @pl.when(step == when)
            def _():
                @pl.loop(first, end)
                def _(t):
                    body(t)

        at(9, reduce_last, 0, EARLY)
        at(8, reduce_fourth, 0, EARLY)
        at(7, reduce_third, 0, EARLY)
        at(6, reduce_second, 0, EARLY)
        late(LAST + 6, finish, LATE, MIDDLE)
        at(7, reduce_last, EARLY)
        at(6, reduce_fourth, EARLY)
        at(5, reduce_third, EARLY)
        at(4, reduce_second, EARLY)
        late(LAST + 4, scatter_fourth, LATE, MIDDLE)
        late(LAST + 5, scatter_fourth, MIDDLE, PAIRS)
        late(LAST + 6, finish, MIDDLE, PAIRS)
        at(2, scatter_second)
        once(EARLY + 3, await_bytes, ring_lower.at[:, :, pl.ds(0, RING - 1)], ring_sem.at[1])
        late(LAST + 3, scatter_turn, LATE, LAST)
        at(3, scatter_third)
        at(3, scatter_turn, 0, LATE)
        at(3, scatter_turn, LAST)
        at(3, correct_early, EARLY)
        at(3, reduce_first, EARLY)
        at(4, scatter_fourth, 0, LATE)
        at(5, finish, 0, LATE)
        at(5, correct, 0, EARLY)
        at(5, reduce_first, 0, EARLY)
        once(0, multiply_first)
        at(0, gather_third, 1)
        at(0, gather_wait, 1)
        at(0, multiply, 1)
        at(0, scatter_first)
        once(-1, prepare)
        at(-1, gather_second)
        at(-2, gather_first)

    for which in range(8):
        ref = gathered.at[:, 0]
        await_bytes(ref.at[:, pl.ds(0, HALF)] if which in (5, 6) else ref, gather_send.at[which])
        buffer = (far, near, far_tile, near_tile)[which // 2]
        await_bytes(buffer.at[:, which % 2], scatter_send.at[which])
    await_bytes(ring_lower.at[:, :, pl.ds(0, RING - 1)], ring_sem.at[0])
    await_bytes(prow_in.at[pl.ds(1, NP - 1)], reduce_send.at[0])
    await_bytes(x_in.at[pl.ds(0, RING - 1)], reduce_send.at[1])
    await_bytes(y_in.at[pl.ds(0, RING - 1)], reduce_send.at[2])
    await_bytes(diag.at[:, pl.ds(0, 224)], reduce_send.at[3])
    await_bytes(panel, out_sem.at[0])
    await_bytes(diag, out_sem.at[1])


def hand_over(panel_in, diag_in, panel_out, diag_out, panel_space, diag_space, sem):
    def parts(panel, diag):
        for k in range(4):
            yield panel.at[pl.ds(k * W // 4, W // 4)]
            yield diag.at[pl.ds(k * 2, 2)]

    stages = [list(parts(*refs)) for refs in (
        (panel_in, diag_in), (panel_space, diag_space), (panel_out, diag_out))]
    loads, stores = (
        [pltpu.make_async_copy(a, b, sem.at[n, k]) for k, (a, b) in enumerate(zip(*stages[n:n + 2]))]
        for n in range(2)
    )
    for load in loads:
        load.start()
    for load, store in zip(loads, stores):
        load.wait()
        store.start()
    for store in stores:
        store.wait()


def on_device(ancestor_inverse, lower_panel, structure, pivot_inverse):
    rows = ancestor_inverse.shape[0]
    blocks = ancestor_inverse.reshape(8, 4, 4, W, W)
    pivot_pairs = pivot_inverse.reshape(PAIRS, COLS, W)
    vmem = pl.BlockSpec(memory_space=pltpu.VMEM)
    hbm = pl.BlockSpec(memory_space=pl.ANY)
    depth = NP * W
    dma = pltpu.SemaphoreType.DMA
    out_shape = (
        jax.ShapeDtypeStruct(lower_panel.shape, F32),
        jax.ShapeDtypeStruct(pivot_pairs.shape, F32),
    )
    panel, diag = pl.pallas_call(
        kernel,
        out_shape=out_shape,
        in_specs=[hbm, hbm, vmem, hbm],
        out_specs=(hbm, hbm),
        scratch_shapes=[
            pltpu.VMEM((rows, depth), BF16),
            pltpu.VMEM((rows, depth), BF16),
            pltpu.VMEM((depth, COLS), BF16),
            pltpu.VMEM((depth, COLS), BF16),
            pltpu.VMEM((16, W), F32),
            pltpu.VMEM((2, RING, 16, W), F32),
            pltpu.VMEM((PAIRS, NP, W, COLS), F32),
            pltpu.VMEM((16, RING, RING, W, W), F32),
            pltpu.VMEM((16, 2, 2, W, W), F32),
            pltpu.VMEM((16, 2, 4, W, W), F32),
            pltpu.VMEM((16, 2, HALF, W), F32),
            pltpu.VMEM((16, 2, W, W), F32),
            pltpu.VMEM((PAIRS, W, COLS), F32),
            pltpu.VMEM((PAIRS, COLS, W), F32),
            pltpu.VMEM((PAIRS - EARLY, 2, RING, W, W), F32),
            pltpu.VMEM((RING, W, W), F32),
            pltpu.VMEM((NP, PAIRS, 32, W), F32),
            pltpu.VMEM((RING, PAIRS, 32, W), F32),
            pltpu.VMEM((RING, PAIRS, 32, W), F32),
            pltpu.VMEM((PAIRS, 32, W), F32),
            pltpu.VMEM((PAIRS, COLS, W), F32),
            dma((4,)),
            dma((2,)),
            dma,
            dma((2,)),
            dma((8,)),
            dma((PAIRS, 7)),
            dma((8,)),
            dma((PAIRS, 4)),
            dma((4,)),
            dma((PAIRS, 4)),
            dma((2,)),
        ],
        compiler_params=pltpu.CompilerParams(
            collective_id=0, has_side_effects=True, vmem_limit_bytes=62 * 1024 * 1024,
        ),
        cost_estimate=pl.CostEstimate(
            flops=2 * 3 * rows * depth * lower_panel.shape[1], bytes_accessed=12 << 20, transcendentals=0,
        ),
    )(blocks, lower_panel, structure, pivot_pairs)
    panel, diag = pl.pallas_call(
        hand_over,
        out_shape=out_shape,
        in_specs=[hbm, hbm],
        out_specs=(hbm, hbm),
        scratch_shapes=[
            pltpu.VMEM(out_shape[0].shape, F32), pltpu.VMEM(out_shape[1].shape, F32), dma((2, 8)),
        ],
        compiler_params=pltpu.CompilerParams(vmem_limit_bytes=62 * 1024 * 1024),
    )(panel, diag)
    return panel, diag.reshape(pivot_inverse.shape)


def solution(mesh):
    return jax.shard_map(
        on_device,
        mesh=mesh,
        in_specs=(P("prow", None, "pcol", None), P(("prow", "pcol"), None), P(), P()),
        out_specs=(P(("prow", "pcol"), None), P()),
        check_vma=False,
    )
```

time: 152 us -> 131 us (0.86)
  Pallas kernels: 146 us -> 130 us
  local copies, waits for them, and re-layouts: 4.59 us -> 0 us
    pallas_call x1 -> x2, Pallas kernels: 146 us -> 130 us  [the longest x1 128 us: on_device(): pl.pallas_call(kernel, out_shape=out_shape, in_specs=[hbm, hbm, vmem, hbm...]
    unnamed x2 -> x0, local copies, waits for them, and re-layouts: 4.59 us -> none
where the time goes in v2:
time: 131 us
  Pallas kernels  130 us (99%)
    pallas_call x1, Pallas kernels, on_device(): pl.pallas_call(kernel, out_shape=out_shape, in_specs=[hbm, hbm, vmem, hbm...  128 us

profile of v2, /device:TPU:1, one launch (start us, length us, event | category | flops | bytes accessed | tf_op | source)
XLA Modules:
  0.0 130.8 jit_solution(6808258301633912920)
XLA Ops:
  0.6 127.8 %shard_map.59 = (f32[128,2048]{1,0:T(8,128)}, f32[8,256,128]{2,1,0:T(8,128)}) custom-call(f32[8,4,4,128,128]{4,3,2,1,0:T(8,128)} %bitcast.3, f32[128,2048]{1,0:T(8,128)} %lower_hbm.1, s32[16,64]{1,0:T(8,128)} %structure_ref.1, f32[8,256,128]{2,1,0:T(8,128)} %bitcast.4), custom_call_target="tpu_custom_call" | custom-call | flops 25769803776 | bytes 12582912 | tf_op jit(solution)/shard_map/pallas_call | solution.py:410
  128.5 2.4 %shard_map.60 = (f32[128,2048]{1,0:T(8,128)}, f32[8,256,128]{2,1,0:T(8,128)}) custom-call(f32[128,2048]{1,0:T(8,128)} %get-tuple-element.6.panel_in, f32[8,256,128]{2,1,0:T(8,128)} %get-tuple-element.7.diag_in), custom_call_target="tpu_custom_call" | custom-call | tf_op jit(solution)/shard_map/pallas_call | solution.py:456

commit v3 on v2

--- a/solution.py
+++ b/solution.py
@@ -131,16 +131,18 @@
             b_high[tile * W:(tile + 1) * W] = high
             b_low[tile * W:(tile + 1) * W] = low
 
-        @pl.loop(0, RING)
-        def _(i):
-            rows = aligned(i * 4 * W, 4 * W)
+    def multiply_rows(h):
+        def body(t):
+            rows = pl.ds(h * 8 * W, 8 * W)
             total = jnp.dot(a_high[rows], b_high[...], preferred_element_type=F32)
             total += jnp.dot(a_low[rows], b_high[...], preferred_element_type=F32)
             total += jnp.dot(a_high[rows], b_low[...], preferred_element_type=F32)
-            for j in range(RING):
-                block = total[j * W:(j + 1) * W]
+            for n in range(8):
+                i, j = h * 2 + n // 4, n % 4
+                block = total[n * W:(n + 1) * W]
                 partial[2 * t, i, j] = block[:, :W]
                 partial[2 * t + 1, j, i] = block[:, W:]
+        return body
 
     def multiply_first():
         @pl.loop(0, RING)
@@ -159,15 +161,17 @@
                 b_high[which * W:(which + 1) * W] = high
                 b_low[which * W:(which + 1) * W] = low
 
-            @pl.loop(0, RING)
-            def _(i):
-                rows = aligned(i * 4 * W, 4 * W)
-                high, low = b_high[0:COLS], b_low[0:COLS]
+            high, low = b_high[0:COLS], b_low[0:COLS]
+
+            @pl.loop(0, 2)
+            def _(h):
+                rows = aligned(h * 8 * W, 8 * W)
                 total = jnp.dot(a_high[rows, depth], high, preferred_element_type=F32)
                 total += jnp.dot(a_low[rows, depth], high, preferred_element_type=F32)
                 total += jnp.dot(a_high[rows, depth], low, preferred_element_type=F32)
-                for j in range(RING):
-                    block = total[j * W:(j + 1) * W]
+                for n in range(8):
+                    i, j = h * 2 + n // 4, n % 4
+                    block = total[n * W:(n + 1) * W]
                     partial[0, i, j] = block[:, :W] + jnp.where(k == 0, 0.0, partial[0, i, j])
                     partial[1, j, i] = block[:, W:] + jnp.where(k == 0, 0.0, partial[1, j, i])
 
@@ -231,8 +235,8 @@
                 precision=lax.Precision.HIGHEST, preferred_element_type=F32,
             )
 
-    def ring_send():
-        for t in range(EARLY, PAIRS):
+    def ring_send(start, end):
+        for t in range(start, end):
             for h, (step, slot) in enumerate(((along_y, y), (along_x, x))):
                 source = gathered.at[t, prow, :, pl.ds(h * W, W)]
                 ring_lower[t - EARLY, h, slot] = source[...]
@@ -249,46 +253,93 @@
                 precision=lax.Precision.HIGHEST, preferred_element_type=F32,
             )
 
-    def reduce_send_to(t, stage, source, target, device):
-        send(source, target, reduce_send.at[stage], reduce_recv.at[t, stage], device)
+    def reduce_send_to(t, stage, source, target, device, sender=None):
+        send(source, target, reduce_send.at[stage if sender is None else sender], reduce_recv.at[t, stage], device)
+
+    def axes(t):
+        even = t % 2 == 0
+        x_devices, y_devices = [along_x(k)[1] for k in range(RING)], [along_y(k)[1] for k in range(RING)]
+        u_devices = [(prow, jnp.where(even, a, b)) for a, b in zip(x_devices, y_devices)]
+        v_devices = [(prow, jnp.where(even, b, a)) for a, b in zip(x_devices, y_devices)]
+        return jnp.where(even, x, y), jnp.where(even, y, x), u_devices, v_devices
 
     def reduce_first(t):
         for k in range(1, NP):
             rows = aligned(((prow + k) % NP) * 32, 32)
             reduce_send_to(t, 0, correction.at[t, rows], prow_in.at[k, t], along_prow(k))
 
-    def reduce_second(t):
+    def sum_prow(t):
         await_bytes(prow_in.at[pl.ds(1, NP - 1), t], reduce_recv.at[t, 0])
         total = correction[t, own_rows]
         for k in range(1, NP):
             total += prow_in[k, t]
-        x_in[x, t] = total
-        for k in range(1, RING):
-            ref = x_in.at[x, t]
-            reduce_send_to(t, 1, ref, ref, along_x(k))
-
-    def reduce_third(t):
-        await_bytes(x_in.at[pl.ds(0, RING - 1), t], reduce_recv.at[t, 1])
-        y_in[y, t] = (x_in[0, t] + x_in[1, t]) + (x_in[2, t] + x_in[3, t])
-        for k in range(1, RING):
-            ref = y_in.at[y, t]
-            reduce_send_to(t, 2, ref, ref, along_y(k))
-
-    def reduce_fourth(t):
-        await_bytes(y_in.at[pl.ds(0, RING - 1), t], reduce_recv.at[t, 2])
-        total = (y_in[0, t] + y_in[1, t]) + (y_in[2, t] + y_in[3, t])
-        diag[t, own_rows] = pivot[t] - total
+        return total
+
+    def spread_prow(t):
         for k in range(1, NP):
             ref = diag.at[t, own_rows]
-            reduce_send_to(t, 3, ref, ref, along_prow(k))
+            reduce_send_to(t, 4, ref, ref, along_prow(k))
+
+    few = pl.ds(0, 8)
+
+    def reduce_second(t):
+        u, v, u_devices, v_devices = axes(t)
+        x_in[0, t] = sum_prow(t)
+        for k in range(1, RING):
+            rows = aligned(((u + k) % RING) * 8, 8)
+            reduce_send_to(t, 1, x_in.at[0, t, rows], x_in.at[k, t, few], u_devices[k])
+
+    def reduce_third(t):
+        u, v, u_devices, v_devices = axes(t)
+        await_bytes(x_in.at[pl.ds(1, RING - 1), t, few], reduce_recv.at[t, 1])
+        total = x_in[0, t, aligned(u * 8, 8)]
+        for k in range(1, RING):
+            total += x_in[k, t, few]
+        y_in[v, t, few] = total
+        for k in range(1, RING):
+            ref = y_in.at[v, t, few]
+            reduce_send_to(t, 2, ref, ref, v_devices[k])
+
+    def reduce_fourth(t):
+        u, v, u_devices, v_devices = axes(t)
+        await_bytes(y_in.at[pl.ds(0, RING - 1), t, few], reduce_recv.at[t, 2])
+        total = (y_in[0, t, few] + y_in[1, t, few]) + (y_in[2, t, few] + y_in[3, t, few])
+        rows = aligned(prow * 32 + u * 8, 8)
+        diag[t, rows] = pivot[t, aligned(u * 8, 8)] - total
+        for k in range(1, RING):
+            ref = diag.at[t, rows]
+            reduce_send_to(t, 3, ref, ref, u_devices[k])
+
+    def reduce_fifth(t):
+        await_bytes(diag.at[t, pl.ds(0, 24)], reduce_recv.at[t, 3])
+        spread_prow(t)
 
     def reduce_last(t):
-        await_bytes(diag.at[t, pl.ds(0, 224)], reduce_recv.at[t, 3])
+        await_bytes(diag.at[t, pl.ds(0, 224)], reduce_recv.at[t, 4])
         pltpu.make_async_copy(diag.at[t], diag_hbm.at[t], out_sem.at[1]).start()
+
+    def last_second():
+        x_in[x, LAST] = sum_prow(LAST)
+        for k in range(1, RING):
+            ref = x_in.at[x, LAST]
+            reduce_send_to(LAST, 1, ref, ref, along_x(k), 5)
+
+    def last_third():
+        await_bytes(x_in.at[pl.ds(0, RING - 1), LAST], reduce_recv.at[LAST, 1])
+        y_in[y, LAST] = (x_in[0, LAST] + x_in[1, LAST]) + (x_in[2, LAST] + x_in[3, LAST])
+        for k in range(1, RING):
+            ref = y_in.at[y, LAST]
+            reduce_send_to(LAST, 2, ref, ref, along_y(k), 6)
+
+    def last_fourth():
+        await_bytes(y_in.at[pl.ds(0, RING - 1), LAST], reduce_recv.at[LAST, 2])
+        total = (y_in[0, LAST] + y_in[1, LAST]) + (y_in[2, LAST] + y_in[3, LAST])
+        diag[LAST, own_rows] = pivot[LAST] - total
+        spread_prow(LAST)
 
     def prepare():
         await_bytes(gathered.at[pl.ds(1, PAIRS - 1), prow], lower_sem.at[1])
-        ring_send()
+        ring_send(EARLY, 6)
 
         @pl.loop(0, 128)
         def _(i):
@@ -327,15 +378,21 @@
                 def _(t):
                     body(t)
 
-        at(9, reduce_last, 0, EARLY)
+        at(10, reduce_last, 0, EARLY)
+        at(9, reduce_fifth, 0, EARLY)
         at(8, reduce_fourth, 0, EARLY)
         at(7, reduce_third, 0, EARLY)
         at(6, reduce_second, 0, EARLY)
         late(LAST + 6, finish, LATE, MIDDLE)
-        at(7, reduce_last, EARLY)
-        at(6, reduce_fourth, EARLY)
-        at(5, reduce_third, EARLY)
-        at(4, reduce_second, EARLY)
+        at(8, reduce_last, EARLY, LAST)
+        at(7, reduce_fifth, EARLY, LAST)
+        at(6, reduce_fourth, EARLY, LAST)
+        at(5, reduce_third, EARLY, LAST)
+        at(4, reduce_second, EARLY, LAST)
+        once(LAST + 7, reduce_last, LAST)
+        once(LAST + 6, last_fourth)
+        once(LAST + 5, last_third)
+        once(LAST + 4, last_second)
         late(LAST + 4, scatter_fourth, LATE, MIDDLE)
         late(LAST + 5, scatter_fourth, MIDDLE, PAIRS)
         late(LAST + 6, finish, MIDDLE, PAIRS)
@@ -355,7 +412,10 @@
         at(0, gather_third, 1)
         at(0, gather_wait, 1)
         at(0, multiply, 1)
+        at(0, multiply_rows(0), 1)
+        at(0, multiply_rows(1), 1)
         at(0, scatter_first)
+        once(0, ring_send, 6, PAIRS)
         once(-1, prepare)
         at(-1, gather_second)
         at(-2, gather_first)
@@ -367,9 +427,12 @@
         await_bytes(buffer.at[:, which % 2], scatter_send.at[which])
     await_bytes(ring_lower.at[:, :, pl.ds(0, RING - 1)], ring_sem.at[0])
     await_bytes(prow_in.at[pl.ds(1, NP - 1)], reduce_send.at[0])
-    await_bytes(x_in.at[pl.ds(0, RING - 1)], reduce_send.at[1])
-    await_bytes(y_in.at[pl.ds(0, RING - 1)], reduce_send.at[2])
-    await_bytes(diag.at[:, pl.ds(0, 224)], reduce_send.at[3])
+    await_bytes(x_in.at[pl.ds(1, RING - 1), pl.ds(0, LAST), few], reduce_send.at[1])
+    await_bytes(y_in.at[pl.ds(0, RING - 1), pl.ds(0, LAST), few], reduce_send.at[2])
+    await_bytes(diag.at[pl.ds(0, LAST), pl.ds(0, 24)], reduce_send.at[3])
+    await_bytes(diag.at[:, pl.ds(0, 224)], reduce_send.at[4])
+    await_bytes(x_in.at[pl.ds(0, RING - 1), LAST], reduce_send.at[5])
+    await_bytes(y_in.at[pl.ds(0, RING - 1), LAST], reduce_send.at[6])
     await_bytes(panel, out_sem.at[0])
     await_bytes(diag, out_sem.at[1])
 
@@ -442,8 +505,8 @@
             dma((PAIRS, 7)),
             dma((8,)),
             dma((PAIRS, 4)),
-            dma((4,)),
-            dma((PAIRS, 4)),
+            dma((7,)),
+            dma((PAIRS, 5)),
             dma((2,)),
         ],
         compiler_params=pltpu.CompilerParams(

time: 131 us -> 126 us (0.962)
  Pallas kernels: 130 us -> 125 us
    pallas_call x1, Pallas kernels: 128 us -> 123 us  [on_device(): pl.pallas_call(kernel, out_shape=out_shape, in_specs=[hbm, hbm, vmem, hbm...]
where the time goes in v3:
time: 126 us
  Pallas kernels  125 us (99%)
    pallas_call x1, Pallas kernels, on_device(): pl.pallas_call(kernel, out_shape=out_shape, in_specs=[hbm, hbm, vmem, hbm...  123 us

profile of v3, /device:TPU:1, one launch (start us, length us, event | category | flops | bytes accessed | tf_op | source)
XLA Modules:
  0.0 126.1 jit_solution(2427219405776289241)
XLA Ops:
  0.6 123.0 %shard_map.59 = (f32[128,2048]{1,0:T(8,128)}, f32[8,256,128]{2,1,0:T(8,128)}) custom-call(f32[8,4,4,128,128]{4,3,2,1,0:T(8,128)} %bitcast.3, f32[128,2048]{1,0:T(8,128)} %lower_hbm.1, s32[16,64]{1,0:T(8,128)} %structure_ref.1, f32[8,256,128]{2,1,0:T(8,128)} %bitcast.4), custom_call_target="tpu_custom_call" | custom-call | flops 25769803776 | bytes 12582912 | tf_op jit(solution)/shard_map/pallas_call | solution.py:473
  123.7 2.4 %shard_map.60 = (f32[128,2048]{1,0:T(8,128)}, f32[8,256,128]{2,1,0:T(8,128)}) custom-call(f32[128,2048]{1,0:T(8,128)} %get-tuple-element.6.panel_in, f32[8,256,128]{2,1,0:T(8,128)} %get-tuple-element.7.diag_in), custom_call_target="tpu_custom_call" | custom-call | tf_op jit(solution)/shard_map/pallas_call | solution.py:519

commit v4 on v3

--- a/solution.py
+++ b/solution.py
@@ -26,6 +26,15 @@
     return high, low
 
 
+def product(left, right):
+    contract = (((0,), (0,)), ((), ()))
+    (left_high, left_low), (right_high, right_low) = split(left), split(right)
+    total = lax.dot_general(left_high, right_high, contract, preferred_element_type=F32)
+    total += lax.dot_general(left_low, right_high, contract, preferred_element_type=F32)
+    total += lax.dot_general(left_high, right_low, contract, preferred_element_type=F32)
+    return total
+
+
 def aligned(start, size):
     return pl.ds(pl.multiple_of(start, size), size)
 
@@ -96,6 +105,7 @@
 
     await_bytes(gathered.at[0, prow], lower_sem.at[0])
     pl.semaphore_wait(barrier, len(partners))
+    await_bytes(gathered.at[pl.ds(1, PAIRS - 1), prow], lower_sem.at[1])
 
     def gather_send_to(t, ref, which, recv, device):
         send(ref, ref, gather_send.at[which], recv, device)
@@ -151,6 +161,8 @@
 
             @pl.when(k == 3)
             def _():
+                gather_second(1)
+                gather_first(2)
                 gather_third(0)
 
             chip = (z + step) % RING
@@ -222,8 +234,8 @@
     def finish(t):
         await_bytes(near_tile.at[pl.ds(2 * t, 2)], scatter_recv.at[t, 3])
         for h, (b, u, v, first, second) in enumerate(routes(t)):
-            product = partial[b, u, v] + near_tile[b, 0] + near_tile[b, 1]
-            panel[t, :, h * W:(h + 1) * W] = -(product * mask[pl.ds(b, 1), :])
+            total = partial[b, u, v] + near_tile[b, 0] + near_tile[b, 1]
+            panel[t, :, h * W:(h + 1) * W] = -(total * mask[pl.ds(b, 1), :])
         columns = aligned(t * COLS, COLS)
         pltpu.make_async_copy(panel.at[t], panel_hbm.at[:, columns], out_sem.at[0]).start()
 
@@ -235,8 +247,8 @@
                 precision=lax.Precision.HIGHEST, preferred_element_type=F32,
             )
 
-    def ring_send(start, end):
-        for t in range(start, end):
+    def ring_send():
+        for t in range(EARLY, PAIRS):
             for h, (step, slot) in enumerate(((along_y, y), (along_x, x))):
                 source = gathered.at[t, prow, :, pl.ds(h * W, W)]
                 ring_lower[t - EARLY, h, slot] = source[...]
@@ -247,10 +259,8 @@
         for h, (b, u, v, first, second) in enumerate(routes(t)):
             for k in range(RING):
                 ring_panel[k] = -(partial[b, u, k] * ring_mask[h, k, pl.ds(b, 1), :])
-            correction[t, h * W:(h + 1) * W] = lax.dot_general(
-                ring_lower[t - EARLY, h].reshape(RING * W, W), ring_panel[...].reshape(RING * W, W),
-                (((0,), (0,)), ((), ())),
-                precision=lax.Precision.HIGHEST, preferred_element_type=F32,
+            correction[t, h * W:(h + 1) * W] = product(
+                ring_lower[t - EARLY, h].reshape(RING * W, W), ring_panel[...].reshape(RING * W, W)
             )
 
     def reduce_send_to(t, stage, source, target, device, sender=None):
@@ -338,8 +348,7 @@
         spread_prow(LAST)
 
     def prepare():
-        await_bytes(gathered.at[pl.ds(1, PAIRS - 1), prow], lower_sem.at[1])
-        ring_send(EARLY, 6)
+        ring_send()
 
         @pl.loop(0, 128)
         def _(i):
@@ -378,6 +387,7 @@
                 def _(t):
                     body(t)
 
+        at(0, gather_third, 1)
         at(10, reduce_last, 0, EARLY)
         at(9, reduce_fifth, 0, EARLY)
         at(8, reduce_fourth, 0, EARLY)
@@ -409,16 +419,16 @@
         at(5, correct, 0, EARLY)
         at(5, reduce_first, 0, EARLY)
         once(0, multiply_first)
-        at(0, gather_third, 1)
         at(0, gather_wait, 1)
         at(0, multiply, 1)
         at(0, multiply_rows(0), 1)
+        at(-1, gather_second, 2)
+        at(-2, gather_first, 3)
         at(0, multiply_rows(1), 1)
         at(0, scatter_first)
-        once(0, ring_send, 6, PAIRS)
+        at(-2, gather_first, 0, 2)
         once(-1, prepare)
-        at(-1, gather_second)
-        at(-2, gather_first)
+        at(-1, gather_second, 0, 1)
 
     for which in range(8):
         ref = gathered.at[:, 0]

time: 126 us -> 125 us (level)
    pallas_call x1, Pallas kernels: 123 us -> 122 us  [on_device(): pl.pallas_call(kernel, out_shape=out_shape, in_specs=[hbm, hbm, vmem, hbm...]
where the time goes in v4:
time: 125 us
  Pallas kernels  124 us (99%)
    pallas_call x1, Pallas kernels, on_device(): pl.pallas_call(kernel, out_shape=out_shape, in_specs=[hbm, hbm, vmem, hbm...  122 us

profile of v4, /device:TPU:1, one launch (start us, length us, event | category | flops | bytes accessed | tf_op | source)
XLA Modules:
  0.0 124.6 jit_solution(6225689408317214925)
XLA Ops:
  0.6 121.6 %shard_map.59 = (f32[128,2048]{1,0:T(8,128)}, f32[8,256,128]{2,1,0:T(8,128)}) custom-call(f32[8,4,4,128,128]{4,3,2,1,0:T(8,128)} %bitcast.3, f32[128,2048]{1,0:T(8,128)} %lower_hbm.1, s32[16,64]{1,0:T(8,128)} %structure_ref.1, f32[8,256,128]{2,1,0:T(8,128)} %bitcast.4), custom_call_target="tpu_custom_call" | custom-call | flops 25769803776 | bytes 12582912 | tf_op jit(solution)/shard_map/pallas_call | solution.py:483
  122.3 2.4 %shard_map.60 = (f32[128,2048]{1,0:T(8,128)}, f32[8,256,128]{2,1,0:T(8,128)}) custom-call(f32[128,2048]{1,0:T(8,128)} %get-tuple-element.6.panel_in, f32[8,256,128]{2,1,0:T(8,128)} %get-tuple-element.7.diag_in), custom_call_target="tpu_custom_call" | custom-call | tf_op jit(solution)/shard_map/pallas_call | solution.py:529

commit v5 on v4

--- a/solution.py
+++ b/solution.py
@@ -196,11 +196,21 @@
     def scatter_send_to(t, which, source, target, device):
         send(source, target, scatter_send.at[which], scatter_recv.at[t, which // 2], device)
 
-    def scatter_first(t):
-        for b, u, v, first, second in routes(t):
+    def scatter_first(t, chosen=(0, 1)):
+        for b, u, v, first, second in [routes(t)[h] for h in chosen]:
             block = partial.at[b, (u + 2) % RING]
             scatter_send_to(t, 0, block.at[pl.ds(0, 2)], far.at[b, 0], first(1))
             scatter_send_to(t, 1, block.at[pl.ds(2, 2)], far.at[b, 1], first(3))
+
+    def scatter_even(ready):
+        def body(t):
+            @pl.when(ready)
+            def _():
+                scatter_first(t, (0,))
+        return body
+
+    def scatter_odd(t):
+        scatter_first(t, (1,))
 
     def scatter_second(t):
         await_bytes(far.at[pl.ds(2 * t, 2)], scatter_recv.at[t, 0])
@@ -241,10 +251,8 @@
 
     def correct(t):
         for h in range(2):
-            correction[t, h * W:(h + 1) * W] = lax.dot_general(
-                gathered[t, prow, :, h * W:(h + 1) * W], panel[t, :, h * W:(h + 1) * W],
-                (((0,), (0,)), ((), ())),
-                precision=lax.Precision.HIGHEST, preferred_element_type=F32,
+            correction[t, h * W:(h + 1) * W] = product(
+                gathered[t, prow, :, h * W:(h + 1) * W], panel[t, :, h * W:(h + 1) * W]
             )
 
     def ring_send():
@@ -422,10 +430,13 @@
         at(0, gather_wait, 1)
         at(0, multiply, 1)
         at(0, multiply_rows(0), 1)
+        at(0, scatter_even(x >= 2), 1)
         at(-1, gather_second, 2)
         at(-2, gather_first, 3)
         at(0, multiply_rows(1), 1)
-        at(0, scatter_first)
+        at(0, scatter_first, 0, 1)
+        at(0, scatter_even(x < 2), 1)
+        at(0, scatter_odd, 1)
         at(-2, gather_first, 0, 2)
         once(-1, prepare)
         at(-1, gather_second, 0, 1)

time: 125 us -> 124 us (level)
  no operation moved by 1% of the time
where the time goes in v5:
time: 124 us
  Pallas kernels  124 us (100%)
    pallas_call x1, Pallas kernels, on_device(): pl.pallas_call(kernel, out_shape=out_shape, in_specs=[hbm, hbm, vmem, hbm...  121 us

profile of v5, /device:TPU:1, one launch (start us, length us, event | category | flops | bytes accessed | tf_op | source)
XLA Modules:
  0.0 124.3 jit_solution(16465012376915987153)
XLA Ops:
  0.6 121.2 %shard_map.59 = (f32[128,2048]{1,0:T(8,128)}, f32[8,256,128]{2,1,0:T(8,128)}) custom-call(f32[8,4,4,128,128]{4,3,2,1,0:T(8,128)} %bitcast.3, f32[128,2048]{1,0:T(8,128)} %lower_hbm.1, s32[16,64]{1,0:T(8,128)} %structure_ref.1, f32[8,256,128]{2,1,0:T(8,128)} %bitcast.4), custom_call_target="tpu_custom_call" | custom-call | flops 25769803776 | bytes 12582912 | tf_op jit(solution)/shard_map/pallas_call | solution.py:494
  121.9 2.4 %shard_map.60 = (f32[128,2048]{1,0:T(8,128)}, f32[8,256,128]{2,1,0:T(8,128)}) custom-call(f32[128,2048]{1,0:T(8,128)} %get-tuple-element.6.panel_in, f32[8,256,128]{2,1,0:T(8,128)} %get-tuple-element.7.diag_in), custom_call_target="tpu_custom_call" | custom-call | tf_op jit(solution)/shard_map/pallas_call | solution.py:540

commit v6 on v4

--- a/solution.py
+++ b/solution.py
@@ -17,7 +17,7 @@
 COLS = 2 * W
 EARLY = 2
 LATE = 2
-MIDDLE = 4
+MIDDLE = 3
 
 
 def split(value):

time: 125 us -> 125 us (level)
  no operation moved by 1% of the time
where the time goes in v6:
time: 125 us; the launch traced here: 124 us
  Pallas kernels  123 us (98%)
    pallas_call x1, Pallas kernels, on_device(): pl.pallas_call(kernel, out_shape=out_shape, in_specs=[hbm, hbm, vmem, hbm...  121 us

profile of v6, /device:TPU:1, one launch (start us, length us, event | category | flops | bytes accessed | tf_op | source)
XLA Modules:
  0.0 124.1 jit_solution(15543749191292723038)
XLA Ops:
  0.6 121.1 %shard_map.59 = (f32[128,2048]{1,0:T(8,128)}, f32[8,256,128]{2,1,0:T(8,128)}) custom-call(f32[8,4,4,128,128]{4,3,2,1,0:T(8,128)} %bitcast.3, f32[128,2048]{1,0:T(8,128)} %lower_hbm.1, s32[16,64]{1,0:T(8,128)} %structure_ref.1, f32[8,256,128]{2,1,0:T(8,128)} %bitcast.4), custom_call_target="tpu_custom_call" | custom-call | flops 25769803776 | bytes 12582912 | tf_op jit(solution)/shard_map/pallas_call | solution.py:483
  121.7 2.4 %shard_map.60 = (f32[128,2048]{1,0:T(8,128)}, f32[8,256,128]{2,1,0:T(8,128)}) custom-call(f32[128,2048]{1,0:T(8,128)} %get-tuple-element.6.panel_in, f32[8,256,128]{2,1,0:T(8,128)} %get-tuple-element.7.diag_in), custom_call_target="tpu_custom_call" | custom-call | tf_op jit(solution)/shard_map/pallas_call | solution.py:529
